TPU v7x, 32 devices: a whole 2x2x4 slice. The times are simulated.
32 devices in a mesh: grp: 2 (over y), ha: 4 (over z), ta: 2 (over x), cam: 2 (over core).
Axes of the slice: x: 2, y: 2, z: 4, core: 2. Of those that a mesh axis runs over, the one named last changes fastest.
Arguments:
- video: bfloat16 [4, 8, 32, 48, 128], P(('grp', 'cam'), 'ta', 'ha'), parts along dimension 0, may hold values from -6 to 6
- norm1_gain: float32 [128], replicated, may hold values from 0.1 to 1.9
- norm1_shift: float32 [128], replicated, may hold values from -3 to 3
- conv1_weight: bfloat16 [3, 3, 3, 128, 128], replicated, may hold values from -0.109375 to 0.109375
- conv1_bias: float32 [128], replicated, may hold values from -3 to 3
- norm2_gain: float32 [128], replicated, may hold values from 0.1 to 1.9
- norm2_shift: float32 [128], replicated, may hold values from -3 to 3
- conv2_weight: bfloat16 [3, 3, 3, 128, 128], replicated, may hold values from -0.109375 to 0.109375
- conv2_bias: float32 [128], replicated, may hold values from -3 to 3
Outputs:
- encoded: bfloat16 [4, 8, 32, 48, 128], P(('grp', 'cam'), 'ta', 'ha'), parts along dimension 0
There are 2 independent parts, one for each index of `grp`. A program takes and returns all parts, laid end to end along the dimension named above; an argument that names none is the same for every part. Nothing has to cross between parts.
All inputs are finite; a program needn't handle non-finite values.
Results may differ from a plain program's by a relative error of at most 0.0039.
Values may be sent and summed in bfloat16 or wider, within the bound.
A program may use at most 128 MiB of HBM per device.

v0:
```python
import jax
import jax.numpy as jnp
from jax import lax
from jax.sharding import PartitionSpec as P


def from_behind(shard, axis, by):
    length = lax.axis_size(axis)
    pairs = [(i, i + by) for i in range(length) if 0 <= i + by < length]
    return lax.ppermute(shard, axis, pairs)


def padded_2(cells, sides, width):
    for axis, dim in sides:
        count = lax.axis_size(axis)
        ends = count - 1
        head = lax.slice_in_dim(cells, 0, width, axis=dim)
        tail = lax.slice_in_dim(cells, cells.shape[dim] - width, cells.shape[dim], axis=dim)
        cells = jnp.concatenate(
            [
                lax.ppermute(tail, axis, [(i, (i + 1) % count) for i in range(ends)]),
                cells,
                lax.ppermute(head, axis, [((i + 1) % count, i) for i in range(ends)]),
            ],
            axis=dim,
        )
    return cells


def activate(values, gain, shift):
    middle = jnp.mean(values, axis=-1, keepdims=True)
    centred = values - middle
    spread = jnp.mean(centred * centred, axis=-1, keepdims=True)
    normed = centred * lax.rsqrt(spread + 1e-06) * gain + shift
    return jax.nn.silu(normed)


def widen(padded):
    return jnp.pad(padded, ((0, 0), (0, 0), (1, 1), (0, 0)))


def conv_valid(padded, weight):
    out_frames = padded.shape[0] - 2
    out_rows = padded.shape[1] - 2
    out_cols = padded.shape[2] - 2
    channels = weight.shape[4]
    summed = jnp.zeros((out_frames, out_rows, out_cols, channels), jnp.float32)
    for step_t in range(3):
        for step_h in range(3):
            for step_w in range(3):
                window = padded[
                    step_t : step_t + out_frames,
                    step_h : step_h + out_rows,
                    step_w : step_w + out_cols,
                ]
                summed = summed + jnp.einsum(
                    "fhwc,cd->fhwd",
                    window,
                    weight[step_t, step_h, step_w],
                    preferred_element_type=jnp.float32,
                )
    return summed


def causal_layer(layer_input, weight, span_index):
    earlier = from_behind(layer_input[-2:], "ta", 1)
    leading = jnp.broadcast_to(layer_input[:1], earlier.shape)
    earlier = jnp.where(span_index == 0, leading, earlier)
    extended = jnp.concatenate([earlier, layer_input], axis=0)
    extended = padded_2(extended, (("ha", 1),), 1)
    return conv_valid(widen(extended), weight)


def body(
    video,
    norm1_gain,
    norm1_shift,
    conv1_weight,
    conv1_bias,
    norm2_gain,
    norm2_shift,
    conv2_weight,
    conv2_bias,
):
    camera_clip = video[0]
    span_index = lax.axis_index("ta")
    inputs = camera_clip.astype(jnp.float32)
    first_input = activate(inputs, norm1_gain, norm1_shift).astype(jnp.bfloat16)
    first_out = causal_layer(first_input, conv1_weight, span_index) + conv1_bias
    second_input = activate(first_out, norm2_gain, norm2_shift).astype(jnp.bfloat16)
    second_out = causal_layer(second_input, conv2_weight, span_index) + conv2_bias
    encoded = (inputs + second_out).astype(jnp.bfloat16)
    return encoded[None]


def solution(mesh):
    placed = (P(("grp", "cam"), "ta", "ha", None, None), P(), P(), P(), P(), P(), P(), P(), P())
    return jax.shard_map(
        body,
        mesh=mesh,
        in_specs=placed,
        out_specs=P(("grp", "cam"), "ta", "ha", None, None),
        check_vma=False,
    )
```

profile of v0, /device:TPU:0, one launch (start us, length us, event | category | flops | bytes accessed | tf_op | source)
XLA Modules:
  0.0 57.1 jit_solution(8246931848457897616)
XLA Ops:
  0.0 1.3 %convert_reduce_fusion = f32[4,8,48]{2,1,0:T(8,128)S(1)} fusion(bf16[1,4,8,48,128]{4,3,2,1,0:T(8,128)(2,1)} %param.9), kind=kLoop, calls=%fused_computation.61 | loop fusion | flops 391680 | bytes 399360 | tf_op jit(solution)/shard_map/reduce_sum | solution.py:31
  1.4 1.5 %fusion.51 = f32[4,8,48]{2,1,0:T(8,128)S(1)} fusion(bf16[1,4,8,48,128]{4,3,2,1,0:T(8,128)(2,1)} %param.9, f32[4,8,48]{2,1,0:T(8,128)S(1)} %broadcast_multiply_fusion.1), kind=kLoop, calls=%fused_computation.78 | loop fusion | flops 784896 | bytes 405504 | tf_op jit(solution)/shard_map/reduce_sum | solution.py:33
  2.9 0.5 fusion.59
  3.5 5.0 %collective-permute-start = (bf16[2,8,48,128]{3,2,1,0:T(8,128)(2,1)S(1)}, bf16[2,8,48,128]{3,2,1,0:T(8,128)(2,1)S(1)}, u32[]{:S(2)}, u32[]{:S(2)}) collective-permute-start(bf16[2,8,48,128]{3,2,1,0:T(8,128)(2,1)S(1)} %slice.495), channel_id=1, source_target_pairs={{0,2},{1,3},{4,6},{5,7},{8,10},{9,11},{12,14},{13,15},{16,18},{17,... | collective-permute-start | bytes 589832 | tf_op jit(solution)/shard_map/ppermute | solution.py:10
  8.5 4.1 %collective-permute-done = bf16[2,8,48,128]{3,2,1,0:T(8,128)(2,1)S(1)} collective-permute-done((bf16[2,8,48,128]{3,2,1,0:T(8,128)(2,1)S(1)}, bf16[2,8,48,128]{3,2,1,0:T(8,128)(2,1)S(1)}, u32[]{:S(2)}, u32[]{:S(2)}) %collective-permute-start) | collective-permute-done | bytes 196640 | tf_op jit(solution)/shard_map/ppermute | solution.py:10
  12.6 3.5 %collective-permute-start.1 = (bf16[6,1,48,128]{3,2,1,0:T(8,128)(2,1)S(1)}, bf16[6,1,48,128]{3,2,1,0:T(8,128)(2,1)S(1)}, u32[]{:S(2)}, u32[]{:S(2)}) collective-permute-start(bf16[6,1,48,128]{3,2,1,0:T(8,128)(2,1)S(1)} %get-tuple-element.7), channel_id=1, source_target_pairs={{0,4},{4,8},{8,12},{1,5},{5,9},{9,13},{2,6},{6,10},{10,14},{3,7},{... | collective-permute-start | bytes 221192 | tf_op jit(solution)/shard_map/ppermute | solution.py:21
  16.1 1.3 %collective-permute-start.2 = (bf16[6,1,48,128]{3,2,1,0:T(8,128)(2,1)S(1)}, bf16[6,1,48,128]{3,2,1,0:T(8,128)(2,1)S(1)}, u32[]{:S(2)}, u32[]{:S(2)}) collective-permute-start(bf16[6,1,48,128]{3,2,1,0:T(8,128)(2,1)S(1)} %get-tuple-element.8), channel_id=1, source_target_pairs={{4,0},{8,4},{12,8},{5,1},{9,5},{13,9},{6,2},{10,6},{14,10},{7,3},{... | collective-permute-start | bytes 221192 | tf_op jit(solution)/shard_map/ppermute | solution.py:23
  17.4 0.6 %fusion.70 = f32[4,8,48,128]{3,2,1,0:T(8,128)S(1)} fusion(bf16[1,4,8,48,128]{4,3,2,1,0:T(8,128)(2,1)S(1)} %copy-done, f32[128]{0:T(128)S(1)} %copy-done.3, f32[128]{0:T(128)S(1)} %copy-done.4, f32[4,8,48]{2,1,0:T(8,128)S(1)} %add_rsqrt_fusion.1, f32[4,8,48]{2,1,0:T(8,128)S(1)} %broadcast_multiply_fusion.1, bf16[3,3,3,128,128]{4,3,2,1,0:T(8,128)(2,1)S(1)} %copy-done.2), kind=kOutput, calls=%fused_computation.105 | convolution fusion | flops 52297728 | bytes 1246208 | tf_op jit(solution)/shard_map/fhwc,cd->fhwd/dot_general | solution.py:56
  18.1 4.3 %collective-permute-done.2 = bf16[6,1,48,128]{3,2,1,0:T(8,128)(2,1)S(1)} collective-permute-done((bf16[6,1,48,128]{3,2,1,0:T(8,128)(2,1)S(1)}, bf16[6,1,48,128]{3,2,1,0:T(8,128)(2,1)S(1)}, u32[]{:S(2)}, u32[]{:S(2)}) %collective-permute-start.2) | collective-permute-done | bytes 73760 | tf_op jit(solution)/shard_map/ppermute | solution.py:23
  22.4 0.4 fusion.48
  23.0 0.3 fusion.133
  23.5 0.3 fusion.129
  24.0 0.3 fusion.125
  24.5 0.3 fusion.121
  25.0 0.3 fusion.117
  25.5 0.3 fusion.109
  26.0 0.3 fusion.113
  26.3 0.3 fusion.105
  26.5 0.3 fusion.197
  27.6 0.3 fusion.35
  27.8 0.3 fusion.33
  28.1 0.3 fusion.31
  28.4 0.3 fusion.29
  28.7 0.3 fusion.27
  29.0 0.4 fusion.25
  29.4 0.3 copy-done.5
  29.6 0.4 fusion.259
  30.1 0.5 multiply_reduce_fusion
  30.7 0.5 multiply_convert_fusion
  31.3 4.5 %collective-permute-start.3 = (bf16[2,8,48,128]{3,2,1,0:T(8,128)(2,1)S(1)}, bf16[2,8,48,128]{3,2,1,0:T(8,128)(2,1)S(1)}, u32[]{:S(2)}, u32[]{:S(2)}) collective-permute-start(bf16[2,8,48,128]{3,2,1,0:T(8,128)(2,1)S(1)} %slice.515), channel_id=1, source_target_pairs={{0,2},{1,3},{4,6},{5,7},{8,10},{9,11},{12,14},{13,15},{16,18},{17,... | collective-permute-start | bytes 589832 | tf_op jit(solution)/shard_map/ppermute | solution.py:10
  35.8 3.1 %collective-permute-done.3 = bf16[2,8,48,128]{3,2,1,0:T(8,128)(2,1)S(1)} collective-permute-done((bf16[2,8,48,128]{3,2,1,0:T(8,128)(2,1)S(1)}, bf16[2,8,48,128]{3,2,1,0:T(8,128)(2,1)S(1)}, u32[]{:S(2)}, u32[]{:S(2)}) %collective-permute-start.3) | collective-permute-done | bytes 196640 | tf_op jit(solution)/shard_map/ppermute | solution.py:10
  39.0 3.5 %collective-permute-start.4 = (bf16[6,1,48,128]{3,2,1,0:T(8,128)(2,1)S(1)}, bf16[6,1,48,128]{3,2,1,0:T(8,128)(2,1)S(1)}, u32[]{:S(2)}, u32[]{:S(2)}) collective-permute-start(bf16[6,1,48,128]{3,2,1,0:T(8,128)(2,1)S(1)} %get-tuple-element.5), channel_id=1, source_target_pairs={{0,4},{4,8},{8,12},{1,5},{5,9},{9,13},{2,6},{6,10},{10,14},{3,7},{... | collective-permute-start | bytes 221192 | tf_op jit(solution)/shard_map/ppermute | solution.py:21
  42.5 1.5 %collective-permute-start.5 = (bf16[6,1,48,128]{3,2,1,0:T(8,128)(2,1)S(1)}, bf16[6,1,48,128]{3,2,1,0:T(8,128)(2,1)S(1)}, u32[]{:S(2)}, u32[]{:S(2)}) collective-permute-start(bf16[6,1,48,128]{3,2,1,0:T(8,128)(2,1)S(1)} %get-tuple-element.6), channel_id=1, source_target_pairs={{4,0},{8,4},{12,8},{5,1},{9,5},{13,9},{6,2},{10,6},{14,10},{7,3},{... | collective-permute-start | bytes 221192 | tf_op jit(solution)/shard_map/ppermute | solution.py:23
  44.5 4.3 %collective-permute-done.5 = bf16[6,1,48,128]{3,2,1,0:T(8,128)(2,1)S(1)} collective-permute-done((bf16[6,1,48,128]{3,2,1,0:T(8,128)(2,1)S(1)}, bf16[6,1,48,128]{3,2,1,0:T(8,128)(2,1)S(1)}, u32[]{:S(2)}, u32[]{:S(2)}) %collective-permute-start.5) | collective-permute-done | bytes 73760 | tf_op jit(solution)/shard_map/ppermute | solution.py:23
  48.8 0.4 select_maximum_fusion
  49.1 0.3 fusion.100
  49.9 0.3 fusion.96
  50.4 0.3 fusion.92
  50.9 0.3 fusion.88
  51.9 0.3 fusion.76
  52.4 0.3 fusion.80
  53.5 0.3 convolution_add_fusion.15
  54.2 0.3 fusion.16
  54.5 0.3 fusion.14
  55.1 0.3 fusion.10
  55.3 0.4 fusion.8
  55.7 0.3 copy-done.8
  56.0 1.1 %fusion.37 = bf16[1,4,8,48,128]{4,3,2,1,0:T(8,128)(2,1)} fusion(f32[4,8,48,128]{3,2,1,0:T(8,128)S(1)} %fusion.72, f32[4,8,48,128]{3,2,1,0:T(8,128)S(1)} %fusion.8, bf16[1,4,8,48,128]{4,3,2,1,0:T(8,128)(2,1)S(1)} %copy-done, f32[128]{0:T(128)S(1)} %copy-done.8, bf16[3,3,3,128,128]{4,3,2,1,0:T(8,128)(2,1)S(1)} %copy-done.1, ...), kind=kOutput, calls=%fused_computation.59 | convolution fusion | flops 53501952 | bytes 3056128 | tf_op jit(solution)/shard_map/fhwc,cd->fhwd/dot_general | solution.py:56
  (55 shorter events, 6.6 us)
Async XLA Ops:
  0.0 2.9 %copy-start = (bf16[1,4,8,48,128]{4,3,2,1,0:T(8,128)(2,1)S(1)}, bf16[1,4,8,48,128]{4,3,2,1,0:T(8,128)(2,1)}, u32[]{:S(2)}) copy-start(bf16[1,4,8,48,128]{4,3,2,1,0:T(8,128)(2,1)} %param.9) | copy-start | bytes 1179652
  0.0 2.9 %copy-start.4 = (f32[128]{0:T(128)S(1)}, f32[128]{0:T(128)}, u32[]{:S(2)}) copy-start(f32[128]{0:T(128)} %param.10) | copy-start | bytes 1540
  0.0 2.9 %copy-start.3 = (f32[128]{0:T(128)S(1)}, f32[128]{0:T(128)}, u32[]{:S(2)}) copy-start(f32[128]{0:T(128)} %param.11) | copy-start | bytes 1540
  3.4 14.0 %copy-start.2 = (bf16[3,3,3,128,128]{4,3,2,1,0:T(8,128)(2,1)S(1)}, bf16[3,3,3,128,128]{4,3,2,1,0:T(8,128)(2,1)}, u32[]{:S(2)}) copy-start(bf16[3,3,3,128,128]{4,3,2,1,0:T(8,128)(2,1)} %param.12) | copy-start | bytes 2654212
  3.5 9.1 %collective-permute-start = (bf16[2,8,48,128]{3,2,1,0:T(8,128)(2,1)S(1)}, bf16[2,8,48,128]{3,2,1,0:T(8,128)(2,1)S(1)}, u32[]{:S(2)}, u32[]{:S(2)}) collective-permute-start(bf16[2,8,48,128]{3,2,1,0:T(8,128)(2,1)S(1)} %slice.495), channel_id=1, source_target_pairs={{0,2},{1,3},{4,6},{5,7},{8,10},{9,11},{12,14},{13,15},{16,18},{17,... | collective-permute-start | bytes 589832 | tf_op jit(solution)/shard_map/ppermute | solution.py:10
  12.6 5.5 %collective-permute-start.1 = (bf16[6,1,48,128]{3,2,1,0:T(8,128)(2,1)S(1)}, bf16[6,1,48,128]{3,2,1,0:T(8,128)(2,1)S(1)}, u32[]{:S(2)}, u32[]{:S(2)}) collective-permute-start(bf16[6,1,48,128]{3,2,1,0:T(8,128)(2,1)S(1)} %get-tuple-element.7), channel_id=1, source_target_pairs={{0,4},{4,8},{8,12},{1,5},{5,9},{9,13},{2,6},{6,10},{10,14},{3,7},{... | collective-permute-start | bytes 221192 | tf_op jit(solution)/shard_map/ppermute | solution.py:21
  16.1 6.2 %collective-permute-start.2 = (bf16[6,1,48,128]{3,2,1,0:T(8,128)(2,1)S(1)}, bf16[6,1,48,128]{3,2,1,0:T(8,128)(2,1)S(1)}, u32[]{:S(2)}, u32[]{:S(2)}) collective-permute-start(bf16[6,1,48,128]{3,2,1,0:T(8,128)(2,1)S(1)} %get-tuple-element.8), channel_id=1, source_target_pairs={{4,0},{8,4},{12,8},{5,1},{9,5},{13,9},{6,2},{10,6},{14,10},{7,3},{... | collective-permute-start | bytes 221192 | tf_op jit(solution)/shard_map/ppermute | solution.py:23
  29.0 0.7 %copy-start.5 = (f32[128]{0:T(128)S(1)}, f32[128]{0:T(128)}, u32[]{:S(2)}) copy-start(f32[128]{0:T(128)} %param.13) | copy-start | bytes 1540
  30.1 0.7 %copy-start.6 = (f32[128]{0:T(128)S(1)}, f32[128]{0:T(128)}, u32[]{:S(2)}) copy-start(f32[128]{0:T(128)} %param.15) | copy-start | bytes 1540
  30.1 0.7 %copy-start.7 = (f32[128]{0:T(128)S(1)}, f32[128]{0:T(128)}, u32[]{:S(2)}) copy-start(f32[128]{0:T(128)} %param.14) | copy-start | bytes 1540
  31.2 12.8 %copy-start.1 = (bf16[3,3,3,128,128]{4,3,2,1,0:T(8,128)(2,1)S(1)}, bf16[3,3,3,128,128]{4,3,2,1,0:T(8,128)(2,1)}, u32[]{:S(2)}) copy-start(bf16[3,3,3,128,128]{4,3,2,1,0:T(8,128)(2,1)} %param.16) | copy-start | bytes 2654212
  31.3 7.7 %collective-permute-start.3 = (bf16[2,8,48,128]{3,2,1,0:T(8,128)(2,1)S(1)}, bf16[2,8,48,128]{3,2,1,0:T(8,128)(2,1)S(1)}, u32[]{:S(2)}, u32[]{:S(2)}) collective-permute-start(bf16[2,8,48,128]{3,2,1,0:T(8,128)(2,1)S(1)} %slice.515), channel_id=1, source_target_pairs={{0,2},{1,3},{4,6},{5,7},{8,10},{9,11},{12,14},{13,15},{16,18},{17,... | collective-permute-start | bytes 589832 | tf_op jit(solution)/shard_map/ppermute | solution.py:10
  39.0 5.5 %collective-permute-start.4 = (bf16[6,1,48,128]{3,2,1,0:T(8,128)(2,1)S(1)}, bf16[6,1,48,128]{3,2,1,0:T(8,128)(2,1)S(1)}, u32[]{:S(2)}, u32[]{:S(2)}) collective-permute-start(bf16[6,1,48,128]{3,2,1,0:T(8,128)(2,1)S(1)} %get-tuple-element.5), channel_id=1, source_target_pairs={{0,4},{4,8},{8,12},{1,5},{5,9},{9,13},{2,6},{6,10},{10,14},{3,7},{... | collective-permute-start | bytes 221192 | tf_op jit(solution)/shard_map/ppermute | solution.py:21
  42.5 6.2 %collective-permute-start.5 = (bf16[6,1,48,128]{3,2,1,0:T(8,128)(2,1)S(1)}, bf16[6,1,48,128]{3,2,1,0:T(8,128)(2,1)S(1)}, u32[]{:S(2)}, u32[]{:S(2)}) collective-permute-start(bf16[6,1,48,128]{3,2,1,0:T(8,128)(2,1)S(1)} %get-tuple-element.6), channel_id=1, source_target_pairs={{4,0},{8,4},{12,8},{5,1},{9,5},{13,9},{6,2},{10,6},{14,10},{7,3},{... | collective-permute-start | bytes 221192 | tf_op jit(solution)/shard_map/ppermute | solution.py:23
  55.3 0.7 %copy-start.8 = (f32[128]{0:T(128)S(1)}, f32[128]{0:T(128)}, u32[]{:S(2)}) copy-start(f32[128]{0:T(128)} %param.17) | copy-start | bytes 1540
where the time goes:
time: 57.4 us; the launch traced here: 57.1 us
  starting transfers between devices  19.3 us (34%)
  waiting for transfers between devices  16.1 us (28%)
  matrix products  15.2 us (26%)
  other arithmetic  5.17 us (9%)
  local copies, waits for them, and re-layouts  0.74 us (1%)
    dot_general x54, matrix products, conv_valid(): jnp.einsum('fhwc,cd->fhwd', window, weight[step_t, step_h, step_w], prefe...  15.2 us
    ppermute x2, starting transfers between devices, from_behind(): return lax.ppermute(shard, axis, pairs)  9.52 us
    ppermute x2, waiting for transfers between devices, padded_2(): lax.ppermute(head, axis, [((i + 1) % count, i) for i in range(ends)])  8.57 us
    ppermute x2, waiting for transfers between devices, from_behind(): return lax.ppermute(shard, axis, pairs)  7.25 us
    ppermute x2, starting transfers between devices, padded_2(): lax.ppermute(tail, axis, [(i, (i + 1) % count) for i in range(ends)])  6.97 us
    ppermute x2, starting transfers between devices, padded_2(): lax.ppermute(head, axis, [((i + 1) % count, i) for i in range(ends)])  2.76 us
    reduce_sum x2, other arithmetic, activate(): spread = jnp.mean(centred * centred, axis=-1, keepdims=True)  2.01 us
    reduce_sum x1, other arithmetic, activate(): middle = jnp.mean(values, axis=-1, keepdims=True)  1.34 us
  transfers between devices with their start and end apart: 6, of which 5 were waited for; matrix products, arithmetic and copies ran while one was open for 2% of the time, Pallas kernels for 0%

commit v1 on v0

v1 whole, which is shorter than its diff:
```python
import functools

import jax
import jax.numpy as jnp
from jax import lax
from jax.experimental import pallas as pl
from jax.experimental.pallas import tpu as pltpu
from jax.sharding import PartitionSpec as P

MESH = pl.DeviceIdType.MESH
F32 = jnp.float32
BF16 = jnp.bfloat16


def activate(values, gain, shift):
    middle = jnp.mean(values, axis=-1, keepdims=True)
    centred = values - middle
    spread = jnp.mean(centred * centred, axis=-1, keepdims=True)
    normed = centred * lax.rsqrt(spread + 1e-06) * gain + shift
    half = 0.5 * normed
    return half + half * jnp.tanh(half)


def spread_columns(cells, width):
    total, channels = cells.shape
    column = lax.rem(lax.broadcasted_iota(jnp.int32, cells.shape, 0), width)
    left = jnp.where(column == 0, 0.0, pltpu.roll(cells, 1, 0))
    right = jnp.where(column == width - 1, 0.0, pltpu.roll(cells, total - 1, 0))
    wide = jnp.concatenate([left.astype(BF16), cells.astype(BF16), right.astype(BF16)], axis=-1)
    return wide.reshape(total // width, width, 3 * channels)


def kernel(
    video, g1, s1, w1, b1, g2, s2, w2, b2,
    out,
    vid, x1, x2, wb1, wb2, mid, obuf,
    vx, vtop, vbot, sx, stop, sbot,
    vsem, wsem, osem, send_v, recv_v, send_s, recv_s,
):
    frames, rows, width, channels = video.shape
    last = rows - 1
    ta, tn = lax.axis_index("ta"), lax.axis_size("ta")
    ha, hn = lax.axis_index("ha"), lax.axis_size("ha")
    has_prev, has_next = ta > 0, ta < tn - 1
    has_up, has_down = ha > 0, ha < hn - 1
    nxt, prv = {"ta": lax.rem(ta + 1, tn)}, {"ta": lax.rem(ta + tn - 1, tn)}
    up, down = {"ha": lax.rem(ha + hn - 1, hn)}, {"ha": lax.rem(ha + 1, hn)}

    barrier = pltpu.get_barrier_semaphore()
    for cond, dev in ((has_next, nxt), (has_prev, prv), (has_up, up), (has_down, down)):
        @pl.when(cond)
        def _():
            pl.semaphore_signal(barrier, inc=1, device_id=dev, device_id_type=MESH)

    vcopy = pltpu.make_async_copy(video, vid, vsem)
    vcopy.start()
    wcopies = []
    for i, (w, wb) in enumerate(((w1, wb1), (w2, wb2))):
        for o in range(2):
            copy = pltpu.make_async_copy(
                w, wb.at[o : o + 3, :, o * channels : (o + 1) * channels], wsem.at[i, o]
            )
            copy.start()
            wcopies.append(copy)
        wb[3, :, 0:channels] = jnp.zeros((wb.shape[1], channels), BF16)
        wb[0, :, channels : 2 * channels] = jnp.zeros((wb.shape[1], channels), BF16)

    amount = (
        has_next.astype(jnp.int32) + has_prev.astype(jnp.int32)
        + has_up.astype(jnp.int32) + has_down.astype(jnp.int32)
    )
    pl.semaphore_wait(barrier, amount)

    def remote(src, dst, sems, k, dev):
        return pltpu.make_async_remote_copy(
            src_ref=src, dst_ref=dst, send_sem=sems[0].at[k], recv_sem=sems[1].at[k],
            device_id=dev, device_id_type=MESH,
        )

    def plan(src, halo, top, bot, sems):
        tail = slice(frames - 2, frames)
        x = [
            remote(src.at[tail, 0], halo.at[:, 0], sems, 0, nxt),
            remote(src.at[tail, last], halo.at[:, last], sems, 1, nxt),
            remote(src.at[tail, 1:last], halo.at[:, 1:last], sems, 2, nxt),
        ]
        forward_up = remote(halo.at[:, 0], bot.at[0:2], sems, 3, up)
        forward_down = remote(halo.at[:, last], top.at[0:2], sems, 4, down)
        late = [
            remote(src.at[tail, 0], bot.at[4:6], sems, 5, up),
            remote(src.at[tail, last], top.at[4:6], sems, 6, down),
        ]
        early = [
            remote(src.at[0:2, 0], bot.at[2:4], sems, 7, up),
            remote(src.at[0:2, last], top.at[2:4], sems, 8, down),
        ]
        return x, (forward_up, forward_down), late, early

    vplan = plan(video, vx, vtop, vbot, (send_v, recv_v))
    splan = plan(mid, sx, stop, sbot, (send_s, recv_s))

    def start_x(p):
        @pl.when(has_next)
        def _():
            for c in p[0]:
                c.start()

    def start_z(pair):
        @pl.when(has_up)
        def _():
            pair[0].start()

        @pl.when(has_down)
        def _():
            pair[1].start()

    def wait_z(pair):
        @pl.when(has_down)
        def _():
            pair[0].wait_recv()

        @pl.when(has_up)
        def _():
            pair[1].wait_recv()

    def forward(p):
        @pl.when(has_prev)
        def _():
            for c in p[0][0:2]:
                c.wait_recv()
            start_z(p[1])

    def wait_forward(p):
        p[0][2].wait_recv()
        wait_z(p[1])

    def finish_sends(p):
        @pl.when(has_next)
        def _():
            for c in p[0]:
                c.wait_send()
        for pair in (p[2], p[3]):
            @pl.when(has_up)
            def _():
                pair[0].wait_send()

            @pl.when(has_down)
            def _():
                pair[1].wait_send()

        @pl.when(has_prev & has_up)
        def _():
            p[1][0].wait_send()

        @pl.when(has_prev & has_down)
        def _():
            p[1][1].wait_send()

    start_z(vplan[2])
    start_x(vplan)
    start_z(vplan[3])

    gain1, shift1 = g1[...].reshape(1, channels), s1[...].reshape(1, channels)
    gain2, shift2 = g2[...].reshape(1, channels), s2[...].reshape(1, channels)
    bias1, bias2 = b1[...].reshape(1, channels), b2[...].reshape(1, channels)
    zero_row = jnp.zeros((width, 3 * channels), BF16)

    def first(cells):
        flat = cells.astype(F32).reshape(-1, channels)
        return spread_columns(activate(flat, gain1, shift1), width)

    def plain(cells):
        return spread_columns(cells.astype(F32).reshape(-1, channels), width)

    def edges(x, top, bot, exts, make):
        for cond, halo, row in ((has_up, top, 0), (has_down, bot, rows + 1)):
            @pl.when(cond)
            def _():
                made = make(halo[exts[0] : exts[-1] + 1])
                for k, e in enumerate(exts):
                    x[e, row] = made[k]

            @pl.when(jnp.logical_not(cond))
            def _():
                for e in exts:
                    x[e, row] = zero_row

    def lead(x, p, halo, top, bot, make):
        @pl.when(has_prev)
        def _():
            wait_forward(p)
            for e in range(2):
                x[e, 1 : rows + 1] = make(halo[e])
            edges(x, top, bot, (0, 1), make)

        @pl.when(jnp.logical_not(has_prev))
        def _():
            for e in range(2):
                x[e] = x[2]

    def conv(x, wb, group, row, count):
        combos = [(r, di) for r in range(4) for di in range(3)]
        depth = 3 * channels
        total = None
        for c in range(0, 12, 2):
            cells = jnp.concatenate(
                [
                    x[2 * group + r, row + di : row + di + count].reshape(count * width, depth)
                    for r, di in combos[c : c + 2]
                ],
                axis=-1,
            )
            weight = jnp.concatenate(
                [wb[r, di * depth : (di + 1) * depth, :] for r, di in combos[c : c + 2]], axis=0
            )
            product = jnp.dot(cells, weight, preferred_element_type=F32)
            total = product if total is None else total + product
        return total

    def conv1(group, row, count):
        summed = conv(x1, wb1, group, row, count)
        for o in range(2):
            part = summed[:, o * channels : (o + 1) * channels] + bias1
            part = activate(part, gain2, shift2)
            frame = 2 * group + o
            mid[frame, row : row + count] = part.astype(BF16).reshape(count, width, channels)
            x2[frame + 2, row + 1 : row + 1 + count] = spread_columns(part, width)

    def conv2(group, row, count):
        summed = conv(x2, wb2, group, row, count)
        for o in range(2):
            part = summed[:, o * channels : (o + 1) * channels] + bias2
            frame = 2 * group + o
            base = vid[frame, row : row + count].astype(F32).reshape(count * width, channels)
            obuf[frame, row : row + count] = (base + part).astype(BF16).reshape(count, width, channels)

    vcopy.wait()
    for f in range(frames):
        x1[f + 2, 1 : rows + 1] = first(vid[f])
    wait_z(vplan[2])
    wait_z(vplan[3])
    edges(x1, vtop, vbot, (2, 3, 4, 5), first)
    forward(vplan)
    wcopies[0].wait()
    wcopies[1].wait()
    conv1(1, 0, rows)
    start_z(splan[2])
    start_x(splan)
    lead(x1, vplan, vx, vtop, vbot, first)
    conv1(0, 0, rows)
    start_z(splan[3])
    wcopies[2].wait()
    wcopies[3].wait()
    forward(splan)
    wait_z(splan[2])
    edges(x2, stop, sbot, (4, 5), plain)
    conv2(1, 1, rows - 2)
    wait_z(splan[3])
    edges(x2, stop, sbot, (2, 3), plain)
    conv2(1, 0, 1)
    conv2(1, last, 1)
    ocopies = [
        pltpu.make_async_copy(obuf.at[2 * g : 2 * g + 2], out.at[2 * g : 2 * g + 2], osem.at[g])
        for g in range(2)
    ]
    ocopies[1].start()
    lead(x2, splan, sx, stop, sbot, plain)
    conv2(0, 0, rows)
    ocopies[0].start()
    finish_sends(vplan)
    finish_sends(splan)
    ocopies[1].wait()
    ocopies[0].wait()


def body(video, g1, s1, w1, b1, g2, s2, w2, b2):
    own = video[0]
    frames, rows, width, channels = own.shape
    flat = (3, 9 * channels, channels)
    hbm = pl.BlockSpec(memory_space=pl.ANY)
    vmem = pl.BlockSpec(memory_space=pltpu.VMEM)
    ext = (frames + 2, rows + 2, width, 3 * channels)
    halo = [
        pltpu.VMEM((2, rows, width, channels), BF16),
        pltpu.VMEM((frames + 2, width, channels), BF16),
        pltpu.VMEM((frames + 2, width, channels), BF16),
    ]
    big = pltpu.VMEM((4, 9 * channels, 2 * channels), BF16)
    own_scratch = pltpu.VMEM(own.shape, BF16)
    dma = pltpu.SemaphoreType.DMA
    result = pl.pallas_call(
        kernel,
        out_shape=jax.ShapeDtypeStruct(own.shape, BF16),
        in_specs=[hbm, vmem, vmem, hbm, vmem, vmem, vmem, hbm, vmem],
        out_specs=hbm,
        scratch_shapes=[
            own_scratch,
            pltpu.VMEM(ext, BF16), pltpu.VMEM(ext, BF16),
            big, big,
            own_scratch, own_scratch,
            *halo, *halo,
            dma(()), dma((2, 2)), dma((2,)),
            dma((9,)), dma((9,)), dma((9,)), dma((9,)),
        ],
        compiler_params=pltpu.CompilerParams(
            collective_id=0, has_side_effects=True, vmem_limit_bytes=56 * 2**20
        ),
        cost_estimate=pl.CostEstimate(
            flops=4 * own.size * 27 * channels,
            bytes_accessed=4 * own.size + 8 * w1.size,
            transcendentals=2 * own.size,
        ),
    )(own, g1, s1, w1.reshape(flat), b1, g2, s2, w2.reshape(flat), b2)
    return result[None]


def solution(mesh):
    placed = (P(("grp", "cam"), "ta", "ha", None, None), P(), P(), P(), P(), P(), P(), P(), P())
    return jax.shard_map(
        body,
        mesh=mesh,
        in_specs=placed,
        out_specs=P(("grp", "cam"), "ta", "ha", None, None),
        check_vma=False,
    )
```

time: 57.4 us -> 21.9 us (0.38)
  Pallas kernels: 0 us -> 19.9 us
  starting transfers between devices: 19.3 us -> 0 us
  waiting for transfers between devices: 16.1 us -> 0 us
  matrix products: 15.2 us -> 0 us
  other arithmetic: 5.17 us -> 0 us
  local copies, waits for them, and re-layouts: 0.74 us -> 1.77 us
    pallas_call x0 -> x1, Pallas kernels: none -> 19.9 us  [body(): pl.pallas_call(kernel, out_shape=jax.ShapeDtypeStruct(own.shape, BF16), i...]
    ppermute x6 -> x0, starting transfers between devices: 19.3 us -> none  [the longest x2 9.52 us: from_behind(): return lax.ppermute(shard, axis, pairs)]
    ppermute x6 -> x0, waiting for transfers between devices: 16.1 us -> none  [the longest x2 8.57 us: padded_2(): lax.ppermute(head, axis, [((i + 1) % count, i) for i in range(ends)])]
    dot_general x54 -> x0, matrix products: 15.2 us -> none  [conv_valid(): jnp.einsum('fhwc,cd->fhwd', window, weight[step_t, step_h, step_w], prefe...]
    reduce_sum x3 -> x0, other arithmetic: 3.35 us -> none  [the longest x2 2.01 us: activate(): spread = jnp.mean(centred * centred, axis=-1, keepdims=True)]
    unnamed x18 -> x1, local copies, waits for them, and re-layouts: 0.7 us -> 1.77 us
    convert_element_type x2 -> x0, other arithmetic: 0.98 us -> none  [the longest x1 0.49 us: body(): first_input = activate(inputs, norm1_gain, norm1_shift).astype(jnp.bfloat16)]
    concatenate x2 -> x0, other arithmetic: 0.74 us -> none  [padded_2(): jnp.concatenate([lax.ppermute(tail, axis, [(i, (i + 1) % count) for i in...]
  transfers between devices with their start and end apart: 6 -> 0, of which waited for: 5 -> 0; matrix products, arithmetic and copies ran while one was open for 2% -> 0% of each run, Pallas kernels for 0% -> 0%
where the time goes in v1:
time: 21.9 us; the launch traced here: 21.7 us
  Pallas kernels  19.9 us (91%)
  local copies, waits for them, and re-layouts  1.77 us (8%)
    pallas_call x1, Pallas kernels, body(): pl.pallas_call(kernel, out_shape=jax.ShapeDtypeStruct(own.shape, BF16), i...  19.9 us
    unnamed x1, local copies, waits for them, and re-layouts  1.77 us

profile of v1, /device:TPU:0, one launch (start us, length us, event | category | flops | bytes accessed | tf_op | source)
XLA Modules:
  0.0 21.7 jit_solution(1737678433298447864)
XLA Ops:
  0.0 19.9 %shard_map.91 = bf16[4,8,48,128]{3,2,1,0:T(8,128)(2,1)} custom-call(bf16[4,8,48,128]{3,2,1,0:T(8,128)(2,1)} %bitcast.7, f32[128]{0:T(128)} %g1.1, f32[128]{0:T(128)} %s1_.1, bf16[3,1152,128]{2,1,0:T(8,128)(2,1)} %bitcast.5, f32[128]{0:T(128)} %b1.1, f32[128]{0:T(128)} %g2.1, f32[128]{0:T(128)} %s2_.1, bf16[3,1152,128]{2,1,0:T(8,128)(2,1)} %bitcast.6, f32[128]{0:T(128)} %b2.1), custom_call_target="tpu_custom_call" | custom-call | flops 2717908992 | bytes 4325376 | tf_op jit(solution)/shard_map/pallas_call | solution.py:291
  19.9 1.8 %copy.11 = bf16[1,4,8,48,128]{4,3,2,1,0:T(8,128)(2,1)} copy(bf16[1,4,8,48,128]{4,3,2,1,0:T(8,128)(2,1)} %bitcast.4) | data formatting | bytes 786432

commit v2 on v1

--- a/solution.py
+++ b/solution.py
@@ -31,11 +31,12 @@
 
 
 def kernel(
-    video, g1, s1, w1, b1, g2, s2, w2, b2,
+    video, hg1, hs1, w1, hb1, hg2, hs2, w2, hb2,
     out,
-    vid, x1, x2, wb1, wb2, mid, obuf,
+    g1, s1, b1, g2, s2, b2,
+    vid, x1, x2, wb1, wb2, mid,
     vx, vtop, vbot, sx, stop, sbot,
-    vsem, wsem, osem, send_v, recv_v, send_s, recv_s,
+    vsem, psem, wsem, send_v, recv_v, send_s, recv_s,
 ):
     frames, rows, width, channels = video.shape
     last = rows - 1
@@ -54,6 +55,10 @@
 
     vcopy = pltpu.make_async_copy(video, vid, vsem)
     vcopy.start()
+    params = ((hg1, g1), (hs1, s1), (hb1, b1), (hg2, g2), (hs2, s2), (hb2, b2))
+    pcopies = [pltpu.make_async_copy(h, v, psem.at[i]) for i, (h, v) in enumerate(params)]
+    for copy in pcopies:
+        copy.start()
     wcopies = []
     for i, (w, wb) in enumerate(((w1, wb1), (w2, wb2))):
         for o in range(2):
@@ -160,6 +165,8 @@
     start_x(vplan)
     start_z(vplan[3])
 
+    for copy in pcopies:
+        copy.wait()
     gain1, shift1 = g1[...].reshape(1, channels), s1[...].reshape(1, channels)
     gain2, shift2 = g2[...].reshape(1, channels), s2[...].reshape(1, channels)
     bias1, bias2 = b1[...].reshape(1, channels), b2[...].reshape(1, channels)
@@ -232,7 +239,7 @@
             part = summed[:, o * channels : (o + 1) * channels] + bias2
             frame = 2 * group + o
             base = vid[frame, row : row + count].astype(F32).reshape(count * width, channels)
-            obuf[frame, row : row + count] = (base + part).astype(BF16).reshape(count, width, channels)
+            out[frame, row : row + count] = (base + part).astype(BF16).reshape(count, width, channels)
 
     vcopy.wait()
     for f in range(frames):
@@ -259,25 +266,18 @@
     edges(x2, stop, sbot, (2, 3), plain)
     conv2(1, 0, 1)
     conv2(1, last, 1)
-    ocopies = [
-        pltpu.make_async_copy(obuf.at[2 * g : 2 * g + 2], out.at[2 * g : 2 * g + 2], osem.at[g])
-        for g in range(2)
-    ]
-    ocopies[1].start()
     lead(x2, splan, sx, stop, sbot, plain)
     conv2(0, 0, rows)
-    ocopies[0].start()
     finish_sends(vplan)
     finish_sends(splan)
-    ocopies[1].wait()
-    ocopies[0].wait()
 
 
 def body(video, g1, s1, w1, b1, g2, s2, w2, b2):
     own = video[0]
+    in_hbm = functools.partial(pltpu.with_memory_space_constraint, memory_space=pltpu.HBM)
     frames, rows, width, channels = own.shape
     flat = (3, 9 * channels, channels)
-    hbm = pl.BlockSpec(memory_space=pl.ANY)
+    hbm = pl.BlockSpec(memory_space=pltpu.HBM)
     vmem = pl.BlockSpec(memory_space=pltpu.VMEM)
     ext = (frames + 2, rows + 2, width, 3 * channels)
     halo = [
@@ -290,27 +290,28 @@
     dma = pltpu.SemaphoreType.DMA
     result = pl.pallas_call(
         kernel,
-        out_shape=jax.ShapeDtypeStruct(own.shape, BF16),
-        in_specs=[hbm, vmem, vmem, hbm, vmem, vmem, vmem, hbm, vmem],
-        out_specs=hbm,
+        out_shape=pltpu.VMEM(own.shape, BF16),
+        in_specs=[hbm] * 9,
+        out_specs=vmem,
         scratch_shapes=[
+            *[pltpu.VMEM((channels,), F32)] * 6,
             own_scratch,
             pltpu.VMEM(ext, BF16), pltpu.VMEM(ext, BF16),
             big, big,
-            own_scratch, own_scratch,
+            own_scratch,
             *halo, *halo,
-            dma(()), dma((2, 2)), dma((2,)),
+            dma(()), dma((6,)), dma((2, 2)),
             dma((9,)), dma((9,)), dma((9,)), dma((9,)),
         ],
         compiler_params=pltpu.CompilerParams(
-            collective_id=0, has_side_effects=True, vmem_limit_bytes=56 * 2**20
+            collective_id=0, has_side_effects=True, vmem_limit_bytes=40 * 2**20
         ),
         cost_estimate=pl.CostEstimate(
             flops=4 * own.size * 27 * channels,
             bytes_accessed=4 * own.size + 8 * w1.size,
             transcendentals=2 * own.size,
         ),
-    )(own, g1, s1, w1.reshape(flat), b1, g2, s2, w2.reshape(flat), b2)
+    )(*[in_hbm(a) for a in (own, g1, s1, w1.reshape(flat), b1, g2, s2, w2.reshape(flat), b2)])
     return result[None]
 
 

time: 21.9 us -> 19.5 us (0.89)
  Pallas kernels: 19.9 us -> 18.6 us
  local copies, waits for them, and re-layouts: 1.77 us -> 0.75 us
    pallas_call x1, Pallas kernels: 19.9 us -> 18.6 us  [body(): pl.pallas_call(kernel, out_shape=pltpu.VMEM(own.shape, BF16), in_specs=[h...]
    unnamed x1, local copies, waits for them, and re-layouts: 1.77 us -> 0.75 us
where the time goes in v2:
time: 19.5 us; the launch traced here: 19.3 us
  Pallas kernels  18.6 us (95%)
  local copies, waits for them, and re-layouts  0.75 us (4%)
    pallas_call x1, Pallas kernels, body(): pl.pallas_call(kernel, out_shape=pltpu.VMEM(own.shape, BF16), in_specs=[h...  18.6 us
    unnamed x1, local copies, waits for them, and re-layouts  0.75 us

profile of v2, /device:TPU:0, one launch (start us, length us, event | category | flops | bytes accessed | tf_op | source)
XLA Modules:
  0.0 19.3 jit_solution(10261123667738412538)
XLA Ops:
  0.0 18.6 %shard_map.91 = bf16[4,8,48,128]{3,2,1,0:T(8,128)(2,1)S(1)} custom-call(bf16[4,8,48,128]{3,2,1,0:T(8,128)(2,1)} %bitcast.7, f32[128]{0:T(128)} %hg1.1, f32[128]{0:T(128)} %hs1.1, bf16[3,1152,128]{2,1,0:T(8,128)(2,1)} %bitcast.5, f32[128]{0:T(128)} %hb1.1, f32[128]{0:T(128)} %hg2.1, f32[128]{0:T(128)} %hs2.1, bf16[3,1152,128]{2,1,0:T(8,128)(2,1)} %bitcast.6, ...), custom_call_target="tpu_custom_call" | custom-call | flops 2717908992 | bytes 4325376 | tf_op jit(solution)/shard_map/pallas_call | solution.py:291
  18.6 0.7 %copy.11 = bf16[1,4,8,48,128]{4,3,2,1,0:T(8,128)(2,1)} copy(bf16[1,4,8,48,128]{4,3,2,1,0:T(8,128)(2,1)S(1)} %bitcast.4) | data formatting | bytes 786432

commit v3 on v2

--- a/solution.py
+++ b/solution.py
@@ -34,7 +34,7 @@
     video, hg1, hs1, w1, hb1, hg2, hs2, w2, hb2,
     out,
     g1, s1, b1, g2, s2, b2,
-    vid, x1, x2, wb1, wb2, mid,
+    vid, x1, x2, wb1, wb2, mid, acc,
     vx, vtop, vbot, sx, stop, sbot,
     vsem, psem, wsem, send_v, recv_v, send_s, recv_s,
 ):
@@ -205,14 +205,20 @@
             for e in range(2):
                 x[e] = x[2]
 
-    def conv(x, wb, group, row, count):
-        combos = [(r, di) for r in range(4) for di in range(3)]
+    def conv(x, wb, group, pieces, steps):
+        combos = [(r, di) for r in steps for di in range(3)]
         depth = 3 * channels
         total = None
-        for c in range(0, 12, 2):
+        for c in range(0, len(combos), 2):
             cells = jnp.concatenate(
                 [
-                    x[2 * group + r, row + di : row + di + count].reshape(count * width, depth)
+                    jnp.concatenate(
+                        [
+                            x[2 * group + r, row + di : row + di + count].reshape(count * width, depth)
+                            for row, count in pieces
+                        ],
+                        axis=0,
+                    )
                     for r, di in combos[c : c + 2]
                 ],
                 axis=-1,
@@ -224,50 +230,64 @@
             total = product if total is None else total + product
         return total
 
-    def conv1(group, row, count):
-        summed = conv(x1, wb1, group, row, count)
+    def cut(block, pieces):
+        start = 0
+        for row, count in pieces:
+            yield row, count, block[start : start + count]
+            start += count
+
+    def finish1(summed, group, pieces):
         for o in range(2):
             part = summed[:, o * channels : (o + 1) * channels] + bias1
             part = activate(part, gain2, shift2)
             frame = 2 * group + o
-            mid[frame, row : row + count] = part.astype(BF16).reshape(count, width, channels)
-            x2[frame + 2, row + 1 : row + 1 + count] = spread_columns(part, width)
-
-    def conv2(group, row, count):
-        summed = conv(x2, wb2, group, row, count)
+            narrow = part.astype(BF16).reshape(-1, width, channels)
+            for row, count, block in cut(narrow, pieces):
+                mid[frame, row : row + count] = block
+            for row, count, block in cut(spread_columns(part, width), pieces):
+                x2[frame + 2, row + 1 : row + 1 + count] = block
+
+    def finish2(summed, group, pieces):
         for o in range(2):
             part = summed[:, o * channels : (o + 1) * channels] + bias2
             frame = 2 * group + o
-            base = vid[frame, row : row + count].astype(F32).reshape(count * width, channels)
-            out[frame, row : row + count] = (base + part).astype(BF16).reshape(count, width, channels)
+            for row, count, block in cut(part.reshape(-1, width, channels), pieces):
+                base = vid[frame, row : row + count].astype(F32)
+                out[frame, row : row + count] = (base + block).astype(BF16)
+
+    whole = [(0, rows)]
+    inner = [(1, rows - 2)]
+    outer = [(0, 1), (last, 1)]
+    every = range(4)
 
     vcopy.wait()
     for f in range(frames):
         x1[f + 2, 1 : rows + 1] = first(vid[f])
+    wcopies[0].wait()
+    wcopies[1].wait()
+    finish1(conv(x1, wb1, 1, inner, every), 1, inner)
     wait_z(vplan[2])
     wait_z(vplan[3])
     edges(x1, vtop, vbot, (2, 3, 4, 5), first)
-    forward(vplan)
-    wcopies[0].wait()
-    wcopies[1].wait()
-    conv1(1, 0, rows)
+    finish1(conv(x1, wb1, 1, outer, every), 1, outer)
     start_z(splan[2])
     start_x(splan)
+    forward(vplan)
+    acc[...] = conv(x1, wb1, 0, whole, (2, 3))
     lead(x1, vplan, vx, vtop, vbot, first)
-    conv1(0, 0, rows)
+    finish1(acc[...] + conv(x1, wb1, 0, whole, (0, 1)), 0, whole)
     start_z(splan[3])
+    forward(splan)
     wcopies[2].wait()
     wcopies[3].wait()
-    forward(splan)
+    finish2(conv(x2, wb2, 1, inner, every), 1, inner)
     wait_z(splan[2])
-    edges(x2, stop, sbot, (4, 5), plain)
-    conv2(1, 1, rows - 2)
     wait_z(splan[3])
-    edges(x2, stop, sbot, (2, 3), plain)
-    conv2(1, 0, 1)
-    conv2(1, last, 1)
+    edges(x2, stop, sbot, (2, 3, 4, 5), plain)
+    finish2(conv(x2, wb2, 1, outer, every), 1, outer)
+    acc[...] = conv(x2, wb2, 0, whole, (2, 3))
     lead(x2, splan, sx, stop, sbot, plain)
-    conv2(0, 0, rows)
+    finish2(acc[...] + conv(x2, wb2, 0, whole, (0, 1)), 0, whole)
     finish_sends(vplan)
     finish_sends(splan)
 
@@ -299,6 +319,7 @@
             pltpu.VMEM(ext, BF16), pltpu.VMEM(ext, BF16),
             big, big,
             own_scratch,
+            pltpu.VMEM((rows * width, 2 * channels), F32),
             *halo, *halo,
             dma(()), dma((6,)), dma((2, 2)),
             dma((9,)), dma((9,)), dma((9,)), dma((9,)),

time: 19.5 us -> 19.9 us (1.021)
  the two profiles are of different devices: /device:TPU:0 before, /device:TPU:6 now
where the time goes in v3:
time: 19.9 us; the launch traced here: 19.8 us
  Pallas kernels  19 us (95%)
  local copies, waits for them, and re-layouts  0.75 us (4%)
    pallas_call x1, Pallas kernels, body(): pl.pallas_call(kernel, out_shape=pltpu.VMEM(own.shape, BF16), in_specs=[h...  19 us
    unnamed x1, local copies, waits for them, and re-layouts  0.75 us

profile of v3, /device:TPU:6, one launch (start us, length us, event | category | flops | bytes accessed | tf_op | source)
XLA Modules:
  0.0 19.8 jit_solution(15761377886119827797)
XLA Ops:
  0.0 19.0 %shard_map.91 = bf16[4,8,48,128]{3,2,1,0:T(8,128)(2,1)S(1)} custom-call(bf16[4,8,48,128]{3,2,1,0:T(8,128)(2,1)} %bitcast.7, f32[128]{0:T(128)} %hg1.1, f32[128]{0:T(128)} %hs1.1, bf16[3,1152,128]{2,1,0:T(8,128)(2,1)} %bitcast.5, f32[128]{0:T(128)} %hb1.1, f32[128]{0:T(128)} %hg2.1, f32[128]{0:T(128)} %hs2.1, bf16[3,1152,128]{2,1,0:T(8,128)(2,1)} %bitcast.6, ...), custom_call_target="tpu_custom_call" | custom-call | flops 2717908992 | bytes 4325376 | tf_op jit(solution)/shard_map/pallas_call | solution.py:311
  19.0 0.7 %copy.11 = bf16[1,4,8,48,128]{4,3,2,1,0:T(8,128)(2,1)} copy(bf16[1,4,8,48,128]{4,3,2,1,0:T(8,128)(2,1)S(1)} %bitcast.4) | data formatting | bytes 786432

commit v4 on v3

--- a/solution.py
+++ b/solution.py
@@ -104,11 +104,23 @@
     vplan = plan(video, vx, vtop, vbot, (send_v, recv_v))
     splan = plan(mid, sx, stop, sbot, (send_s, recv_s))
 
-    def start_x(p):
+    def start_x_edges(p):
         @pl.when(has_next)
         def _():
-            for c in p[0]:
+            for c in p[0][0:2]:
                 c.start()
+
+    def start_x_inner(p):
+        @pl.when(has_next)
+        def _():
+            for c in p[0][0:2]:
+                c.wait_send()
+            p[0][2].start()
+
+    def wait_x_inner(p):
+        @pl.when(has_next)
+        def _():
+            p[0][2].wait_send()
 
     def start_z(pair):
         @pl.when(has_up)
@@ -140,10 +152,6 @@
         wait_z(p[1])
 
     def finish_sends(p):
-        @pl.when(has_next)
-        def _():
-            for c in p[0]:
-                c.wait_send()
         for pair in (p[2], p[3]):
             @pl.when(has_up)
             def _():
@@ -161,8 +169,8 @@
         def _():
             p[1][1].wait_send()
 
+    start_x_edges(vplan)
     start_z(vplan[2])
-    start_x(vplan)
     start_z(vplan[3])
 
     for copy in pcopies:
@@ -263,17 +271,20 @@
     vcopy.wait()
     for f in range(frames):
         x1[f + 2, 1 : rows + 1] = first(vid[f])
+    start_x_inner(vplan)
     wcopies[0].wait()
     wcopies[1].wait()
     finish1(conv(x1, wb1, 1, inner, every), 1, inner)
     wait_z(vplan[2])
     wait_z(vplan[3])
+    forward(vplan)
     edges(x1, vtop, vbot, (2, 3, 4, 5), first)
     finish1(conv(x1, wb1, 1, outer, every), 1, outer)
     start_z(splan[2])
-    start_x(splan)
-    forward(vplan)
+    wait_x_inner(vplan)
+    start_x_edges(splan)
     acc[...] = conv(x1, wb1, 0, whole, (2, 3))
+    start_x_inner(splan)
     lead(x1, vplan, vx, vtop, vbot, first)
     finish1(acc[...] + conv(x1, wb1, 0, whole, (0, 1)), 0, whole)
     start_z(splan[3])
@@ -288,6 +299,7 @@
     acc[...] = conv(x2, wb2, 0, whole, (2, 3))
     lead(x2, splan, sx, stop, sbot, plain)
     finish2(acc[...] + conv(x2, wb2, 0, whole, (0, 1)), 0, whole)
+    wait_x_inner(splan)
     finish_sends(vplan)
     finish_sends(splan)
 

time: 19.9 us -> 19.4 us (0.975)
  the two profiles are of different devices: /device:TPU:6 before, /device:TPU:0 now
where the time goes in v4:
time: 19.4 us; the launch traced here: 19.3 us
  Pallas kernels  18.5 us (95%)
  local copies, waits for them, and re-layouts  0.75 us (4%)
    pallas_call x1, Pallas kernels, body(): pl.pallas_call(kernel, out_shape=pltpu.VMEM(own.shape, BF16), in_specs=[h...  18.5 us
    unnamed x1, local copies, waits for them, and re-layouts  0.75 us

profile of v4, /device:TPU:0, one launch (start us, length us, event | category | flops | bytes accessed | tf_op | source)
XLA Modules:
  0.0 19.3 jit_solution(13640241512741679495)
XLA Ops:
  0.0 18.5 %shard_map.91 = bf16[4,8,48,128]{3,2,1,0:T(8,128)(2,1)S(1)} custom-call(bf16[4,8,48,128]{3,2,1,0:T(8,128)(2,1)} %bitcast.7, f32[128]{0:T(128)} %hg1.1, f32[128]{0:T(128)} %hs1.1, bf16[3,1152,128]{2,1,0:T(8,128)(2,1)} %bitcast.5, f32[128]{0:T(128)} %hb1.1, f32[128]{0:T(128)} %hg2.1, f32[128]{0:T(128)} %hs2.1, bf16[3,1152,128]{2,1,0:T(8,128)(2,1)} %bitcast.6, ...), custom_call_target="tpu_custom_call" | custom-call | flops 2717908992 | bytes 4325376 | tf_op jit(solution)/shard_map/pallas_call | solution.py:323
  18.5 0.7 %copy.11 = bf16[1,4,8,48,128]{4,3,2,1,0:T(8,128)(2,1)} copy(bf16[1,4,8,48,128]{4,3,2,1,0:T(8,128)(2,1)S(1)} %bitcast.4) | data formatting | bytes 786432

commit v5 on v4

--- a/solution.py
+++ b/solution.py
@@ -281,13 +281,13 @@
     edges(x1, vtop, vbot, (2, 3, 4, 5), first)
     finish1(conv(x1, wb1, 1, outer, every), 1, outer)
     start_z(splan[2])
+    acc[...] = conv(x1, wb1, 0, whole, (2, 3))
     wait_x_inner(vplan)
     start_x_edges(splan)
-    acc[...] = conv(x1, wb1, 0, whole, (2, 3))
-    start_x_inner(splan)
     lead(x1, vplan, vx, vtop, vbot, first)
     finish1(acc[...] + conv(x1, wb1, 0, whole, (0, 1)), 0, whole)
     start_z(splan[3])
+    start_x_inner(splan)
     forward(splan)
     wcopies[2].wait()
     wcopies[3].wait()

time: 19.4 us -> 18.3 us (0.943)
  Pallas kernels: 18.5 us -> 17.2 us
    pallas_call x1, Pallas kernels: 18.5 us -> 17.2 us  [body(): pl.pallas_call(kernel, out_shape=pltpu.VMEM(own.shape, BF16), in_specs=[h...]
where the time goes in v5:
time: 18.3 us; the launch traced here: 18 us
  Pallas kernels  17.2 us (94%)
  local copies, waits for them, and re-layouts  0.75 us (4%)
    pallas_call x1, Pallas kernels, body(): pl.pallas_call(kernel, out_shape=pltpu.VMEM(own.shape, BF16), in_specs=[h...  17.2 us
    unnamed x1, local copies, waits for them, and re-layouts  0.75 us

profile of v5, /device:TPU:0, one launch (start us, length us, event | category | flops | bytes accessed | tf_op | source)
XLA Modules:
  0.0 18.0 jit_solution(1679987767669977179)
XLA Ops:
  0.0 17.2 %shard_map.91 = bf16[4,8,48,128]{3,2,1,0:T(8,128)(2,1)S(1)} custom-call(bf16[4,8,48,128]{3,2,1,0:T(8,128)(2,1)} %bitcast.7, f32[128]{0:T(128)} %hg1.1, f32[128]{0:T(128)} %hs1.1, bf16[3,1152,128]{2,1,0:T(8,128)(2,1)} %bitcast.5, f32[128]{0:T(128)} %hb1.1, f32[128]{0:T(128)} %hg2.1, f32[128]{0:T(128)} %hs2.1, bf16[3,1152,128]{2,1,0:T(8,128)(2,1)} %bitcast.6, ...), custom_call_target="tpu_custom_call" | custom-call | flops 2717908992 | bytes 4325376 | tf_op jit(solution)/shard_map/pallas_call | solution.py:323
  17.3 0.7 %copy.11 = bf16[1,4,8,48,128]{4,3,2,1,0:T(8,128)(2,1)} copy(bf16[1,4,8,48,128]{4,3,2,1,0:T(8,128)(2,1)S(1)} %bitcast.4) | data formatting | bytes 786432

commit v6 on v5

--- a/solution.py
+++ b/solution.py
@@ -147,10 +147,6 @@
                 c.wait_recv()
             start_z(p[1])
 
-    def wait_forward(p):
-        p[0][2].wait_recv()
-        wait_z(p[1])
-
     def finish_sends(p):
         for pair in (p[2], p[3]):
             @pl.when(has_up)
@@ -203,10 +199,15 @@
     def lead(x, p, halo, top, bot, make):
         @pl.when(has_prev)
         def _():
-            wait_forward(p)
+            wait_z(p[1])
+            for row in (0, last):
+                made = make(halo[:, row])
+                for e in range(2):
+                    x[e, row + 1] = made[e]
+            edges(x, top, bot, (0, 1), make)
+            p[0][2].wait_recv()
             for e in range(2):
-                x[e, 1 : rows + 1] = make(halo[e])
-            edges(x, top, bot, (0, 1), make)
+                x[e, 2:rows] = make(halo[e, 1:last])
 
         @pl.when(jnp.logical_not(has_prev))
         def _():
@@ -244,8 +245,10 @@
             yield row, count, block[start : start + count]
             start += count
 
-    def finish1(summed, group, pieces):
+    def finish1(summed, group, pieces, between=None):
         for o in range(2):
+            if o == 1 and between is not None:
+                between()
             part = summed[:, o * channels : (o + 1) * channels] + bias1
             part = activate(part, gain2, shift2)
             frame = 2 * group + o
@@ -285,9 +288,8 @@
     wait_x_inner(vplan)
     start_x_edges(splan)
     lead(x1, vplan, vx, vtop, vbot, first)
-    finish1(acc[...] + conv(x1, wb1, 0, whole, (0, 1)), 0, whole)
+    finish1(acc[...] + conv(x1, wb1, 0, whole, (0, 1)), 0, whole, lambda: start_x_inner(splan))
     start_z(splan[3])
-    start_x_inner(splan)
     forward(splan)
     wcopies[2].wait()
     wcopies[3].wait()

time: 18.3 us -> 19.1 us (1.044)
  Pallas kernels: 17.2 us -> 18.2 us
    pallas_call x1, Pallas kernels: 17.2 us -> 18.2 us  [body(): pl.pallas_call(kernel, out_shape=pltpu.VMEM(own.shape, BF16), in_specs=[h...]
where the time goes in v6:
time: 19.1 us; the launch traced here: 18.9 us
  Pallas kernels  18.2 us (95%)
  local copies, waits for them, and re-layouts  0.75 us (4%)
    pallas_call x1, Pallas kernels, body(): pl.pallas_call(kernel, out_shape=pltpu.VMEM(own.shape, BF16), in_specs=[h...  18.2 us
    unnamed x1, local copies, waits for them, and re-layouts  0.75 us

profile of v6, /device:TPU:0, one launch (start us, length us, event | category | flops | bytes accessed | tf_op | source)
XLA Modules:
  0.0 18.9 jit_solution(13646079939555609540)
XLA Ops:
  0.0 18.2 %shard_map.91 = bf16[4,8,48,128]{3,2,1,0:T(8,128)(2,1)S(1)} custom-call(bf16[4,8,48,128]{3,2,1,0:T(8,128)(2,1)} %bitcast.7, f32[128]{0:T(128)} %hg1.1, f32[128]{0:T(128)} %hs1.1, bf16[3,1152,128]{2,1,0:T(8,128)(2,1)} %bitcast.5, f32[128]{0:T(128)} %hb1.1, f32[128]{0:T(128)} %hg2.1, f32[128]{0:T(128)} %hs2.1, bf16[3,1152,128]{2,1,0:T(8,128)(2,1)} %bitcast.6, ...), custom_call_target="tpu_custom_call" | custom-call | flops 2717908992 | bytes 4325376 | tf_op jit(solution)/shard_map/pallas_call | solution.py:325
  18.2 0.7 %copy.11 = bf16[1,4,8,48,128]{4,3,2,1,0:T(8,128)(2,1)} copy(bf16[1,4,8,48,128]{4,3,2,1,0:T(8,128)(2,1)S(1)} %bitcast.4) | data formatting | bytes 786432
